TPU v7x, 512 devices: a whole 4x8x8 slice. The times are simulated.
512 devices in a mesh: gz: 4 (over x), gy: 16 (over z, y_hi), gx: 8 (over y_lo, core).
Axes of the slice: x: 4, y: 8 (y_hi: 2, y_lo: 4; y = y_hi * 4 + y_lo), z: 8, core: 2. Of those that a mesh axis runs over, the one named last changes fastest.
Arguments:
- volume: bfloat16 [32, 16, 128, 384], P('gz', 'gy', 'gx'), may hold values from -80 to 80
- cotangent: bfloat16 [32, 16, 128, 384], P('gz', 'gy', 'gx'), may hold values from -6 to 6
- w_project: bfloat16 [3, 384, 1152], P(None, 'gy', ('gz', 'gx')), may hold values from -0.3125 to 0.3125
- w_output: bfloat16 [3, 384, 384], P(None, 'gy', ('gz', 'gx')), may hold values from -0.3125 to 0.3125
Outputs:
- grad_volume: bfloat16 [32, 16, 128, 384], P('gz', 'gy', 'gx')
All inputs are finite; a program needn't handle non-finite values.
Results may differ from a plain program's by a relative error of at most 0.015.
Values may be sent and summed in bfloat16 or wider, within the bound.
A program may use at most 64 MiB of HBM per device.

v0:
```python
import jax
import jax.numpy as jnp
from jax import lax
from jax.sharding import PartitionSpec as P

HEADS = 6


def head_norm(vector):
    return (vector * lax.rsqrt(jnp.mean(vector * vector, axis=-1, keepdims=True) + 1e-06)).astype(
        jnp.bfloat16
    )


def sublayer(line_rows, w_inner, w_outer):
    feat_len = line_rows.shape[-1]
    head_size = feat_len // HEADS
    stream = line_rows.astype(jnp.float32)
    normed = (stream * lax.rsqrt(jnp.mean(stream * stream, axis=-1, keepdims=True) + 1e-06)).astype(
        jnp.bfloat16
    )
    packed = jnp.dot(normed, w_inner, preferred_element_type=jnp.float32)
    head_shape = line_rows.shape[:3] + (HEADS, head_size)
    queries = head_norm(packed[..., :feat_len].reshape(head_shape))
    key_part = head_norm(packed[..., feat_len : 2 * feat_len].reshape(head_shape))
    value_part = packed[..., 2 * feat_len :].reshape(head_shape).astype(jnp.bfloat16)
    scores = jnp.einsum(
        "plqhe,pkqhe->pqhlk", queries, key_part, preferred_element_type=jnp.float32
    ) * head_size ** (-0.5)
    powers = jnp.exp(scores)
    attn_weights = (powers / jnp.sum(powers, axis=-1, keepdims=True)).astype(jnp.bfloat16)
    mixed_out = jnp.einsum(
        "pqhlk,pkqhe->plqhe", attn_weights, value_part, preferred_element_type=jnp.float32
    )
    mixed_out = mixed_out.astype(jnp.bfloat16).reshape(line_rows.shape)
    update = jnp.dot(mixed_out, w_outer, preferred_element_type=jnp.float32)
    return (stream + update).astype(jnp.bfloat16)


def along_depth(member, w_inner, w_outer):
    depth_len, row_len, rest_len, feat_len = member.shape
    flat_lines = member.reshape(1, depth_len, row_len * rest_len, feat_len)
    return sublayer(flat_lines, w_inner, w_outer).reshape(member.shape)


def along_rows(member, w_inner, w_outer):
    return sublayer(member, w_inner, w_outer)


def along_columns(member, w_inner, w_outer):
    depth_len, row_len, col_len, feat_len = member.shape
    flat_lines = member.reshape(depth_len * row_len, col_len, 1, feat_len)
    return sublayer(flat_lines, w_inner, w_outer).reshape(member.shape)


def backward_pass(local_fn, activ_lines, grad_lines):
    _, pullback = jax.vjp(local_fn, activ_lines)
    return pullback(grad_lines)[0]


def depth_out(stacked):
    return lax.all_to_all(stacked, "gz", split_axis=3, concat_axis=1, tiled=True)


def depth_in(stacked):
    return lax.all_to_all(stacked, "gz", split_axis=1, concat_axis=3, tiled=True)


def rows_out(stacked):
    return lax.all_to_all(stacked, "gy", split_axis=3, concat_axis=2, tiled=True)


def rows_in(stacked):
    return lax.all_to_all(stacked, "gy", split_axis=2, concat_axis=3, tiled=True)


def columns_out(stacked):
    return lax.all_to_all(stacked, "gx", split_axis=1, concat_axis=3, tiled=True)


def columns_in(stacked):
    return lax.all_to_all(stacked, "gx", split_axis=3, concat_axis=1, tiled=True)


def local(volume, cotangent, w_project, w_output):
    part_proj, part_outp = (
        lax.all_gather(w_project, "gy", axis=1, tiled=True),
        lax.all_gather(w_output, "gy", axis=1, tiled=True),
    )
    proj_full, outp_full = (
        lax.all_gather(part_proj, ("gz", "gx"), axis=2, tiled=True),
        lax.all_gather(part_outp, ("gz", "gx"), axis=2, tiled=True),
    )

    def depth_fn(member):
        return along_depth(member, proj_full[0], outp_full[0])

    def row_fn(member):
        return along_rows(member, proj_full[1], outp_full[1])

    def column_fn(member):
        return along_columns(member, proj_full[2], outp_full[2])

    depth_act = depth_out(volume[None])[0]
    field_one = depth_in(depth_fn(depth_act)[None])[0]
    row_act = rows_out(field_one[None])[0]
    field_two = rows_in(row_fn(row_act)[None])[0]
    paired = columns_out(jnp.stack([cotangent, field_two]))
    grad_two = columns_in(backward_pass(column_fn, paired[1], paired[0])[None])[0]
    row_grad = rows_out(grad_two[None])[0]
    grad_one = rows_in(backward_pass(row_fn, row_act, row_grad)[None])[0]
    depth_grad = depth_out(grad_one[None])[0]
    grad_zero = depth_in(backward_pass(depth_fn, depth_act, depth_grad)[None])[0]
    return grad_zero


def solution(mesh):
    return jax.shard_map(
        local,
        mesh=mesh,
        in_specs=(
            P("gz", "gy", "gx", None),
            P("gz", "gy", "gx", None),
            P(None, "gy", ("gz", "gx")),
            P(None, "gy", ("gz", "gx")),
        ),
        out_specs=P("gz", "gy", "gx", None),
        check_vma=False,
    )
```

profile of v0, /device:TPU:1, one launch (start us, length us, event | category | flops | bytes accessed | tf_op | source)
XLA Modules:
  0.0 389.5 jit_solution(16823978109501460012)
XLA Ops:
  6.5 55.6 %all_gather.12 = bf16[3,384,36]{2,1,0:T(8,128)(2,1)S(1)} all-gather(bf16[3,24,36]{2,1,0:T(8,128)(2,1)} %param.6), channel_id=1, replica_groups=mesh['gz'=4,'gy'=16,'gx'=8] {'gy'}, dimensions={1}, use_global_device_ids=true | all-gather | bytes 88128 | tf_op jit(solution)/shard_map/all_gather | solution.py:87
  64.5 4.0 %all-to-all-start = ((bf16[1,8,1,16,384]{4,1,2,0,3:T(8,128)(2,1)}), bf16[1,8,1,16,384]{4,1,2,0,3:T(8,128)(2,1)S(1)}, u32[]{:S(2)}, u32[]{:S(2)}) async-start(bf16[1,8,1,16,384]{4,1,2,0,3:T(8,128)(2,1)} %bitcast.315), calls=%async_computation | async-start | bytes 196608 | tf_op jit(solution)/shard_map/all_to_all | solution.py:62
  69.4 47.6 %all_gather.14 = bf16[3,384,12]{2,0,1:T(4,128)(2,1)S(1)} all-gather(bf16[3,24,12]{2,0,1:T(4,128)(2,1)S(1)} %copy.345), channel_id=1, replica_groups=mesh['gz'=4,'gy'=16,'gx'=8] {'gy'}, dimensions={1}, use_global_device_ids=true | all-gather | bytes 29376 | tf_op jit(solution)/shard_map/all_gather | solution.py:88
  117.2 62.5 %all_gather.15 = bf16[3,384,384]{1,0,2:T(4,128)(2,1)S(1)} all-gather(bf16[3,384,12]{1,0,2:T(4,128)(2,1)S(1)} %copy.346), channel_id=1, replica_groups=mesh['gz'=4,'gy'=16,'gx'=8] {'gz','gx'}, dimensions={2}, use_global_device_ids=true | all-gather | bytes 912384 | tf_op jit(solution)/shard_map/all_gather | solution.py:92
  179.7 2.3 fusion.130
  184.5 9.5 %fusion.129 = (bf16[1,384,1152]{1,0,2:T(2,128)(2,1)S(1)}, bf16[1,384,1152]{1,0,2:T(2,128)(2,1)S(1)}, bf16[1,384,1152]{1,0,2:T(2,128)(2,1)}) fusion(bf16[3,384,1152]{1,0,2:T(4,128)(2,1)} %all-gather.2.cloned.1.call-done), kind=kLoop, calls=%fused_computation.229 | loop fusion | bytes 5308416 | tf_op jit(solution)/shard_map/jvp()/slice | solution.py:102
  194.0 4.8 %copy.429 = bf16[1,384,1152]{2,1,0:T(8,128)(2,1)} copy(bf16[1,384,1152]{1,0,2:T(2,128)(2,1)} %get-tuple-element.7) | data formatting | bytes 1769472
  201.9 1.9 reshape.989
  203.7 1.8 reshape.988
  205.6 1.8 reshape.991
  207.4 1.8 reshape.990
  211.1 1.9 multiply_reduce_fusion.3
  215.9 1.9 multiply_reduce_fusion.2
  228.9 7.0 %all_to_all.120 = bf16[1,32,1,4,384]{4,3,2,0,1:T(4,128)(2,1)S(1)} all-to-all(bf16[1,32,1,4,384]{4,3,2,0,1:T(4,128)(2,1)S(1)} %copy.348), channel_id=1, replica_groups=mesh['gz'=4,'gy'=16,'gx'=8] {'gz'}, dimensions={1} | all-to-all | bytes 196608 | tf_op jit(solution)/shard_map/all_to_all | solution.py:66
  236.6 7.7 %all-to-all-start.2 = ((bf16[1,8,1,16,384]{4,1,2,0,3:T(8,128)(2,1)}), bf16[1,8,1,16,384]{4,1,2,0,3:T(8,128)(2,1)}, u32[]{:S(2)}, u32[]{:S(2)}) async-start(bf16[1,8,1,16,384]{4,1,2,0,3:T(8,128)(2,1)} %bitcast.343), calls=%async_computation.2 | async-start | bytes 196608 | tf_op jit(solution)/shard_map/all_to_all | solution.py:70
  244.3 2.8 copy.432
  247.1 3.7 copy.431
  250.8 5.2 %all-to-all-done.2 = bf16[1,8,1,16,384]{4,1,2,0,3:T(8,128)(2,1)} async-done(((bf16[1,8,1,16,384]{4,1,2,0,3:T(8,128)(2,1)}), bf16[1,8,1,16,384]{4,1,2,0,3:T(8,128)(2,1)}, u32[]{:S(2)}, u32[]{:S(2)}) %all-to-all-start.2) | async-done | bytes 98336 | tf_op jit(solution)/shard_map/all_to_all | solution.py:70
  269.7 6.2 %all-to-all-start.3 = ((bf16[1,8,16,1,384]{4,1,3,0,2:T(8,128)(2,1)}), bf16[1,8,16,1,384]{4,1,3,0,2:T(8,128)(2,1)S(1)}, u32[]{:S(2)}, u32[]{:S(2)}) async-start(bf16[1,8,16,1,384]{4,1,3,0,2:T(8,128)(2,1)} %copy.362), calls=%async_computation.3 | async-start | bytes 196608 | tf_op jit(solution)/shard_map/all_to_all | solution.py:74
  276.8 10.8 %all-to-all-done.3 = bf16[1,8,16,1,384]{4,1,3,0,2:T(8,128)(2,1)S(1)} async-done(((bf16[1,8,16,1,384]{4,1,3,0,2:T(8,128)(2,1)}), bf16[1,8,16,1,384]{4,1,3,0,2:T(8,128)(2,1)S(1)}, u32[]{:S(2)}, u32[]{:S(2)}) %all-to-all-start.3) | async-done | bytes 98336 | tf_op jit(solution)/shard_map/all_to_all | solution.py:74
  288.3 6.6 %all-to-all-start.4 = ((bf16[2,8,1,16,384]{4,3,2,0,1:T(8,128)(2,1)}), bf16[2,8,1,16,384]{4,3,2,0,1:T(8,128)(2,1)S(1)}, u32[]{:S(2)}, u32[]{:S(2)}) async-start(bf16[2,8,1,16,384]{4,3,2,0,1:T(8,128)(2,1)} %copy.363), calls=%async_computation.4 | async-start | bytes 393216 | tf_op jit(solution)/shard_map/all_to_all | solution.py:78
  294.9 2.8 copy.433
  297.7 3.8 copy.434
  309.7 5.1 %all-to-all-start.5 = ((bf16[8,2,3072]{2,1,0:T(2,128)(2,1)}), bf16[8,2,3072]{2,1,0:T(2,128)(2,1)S(1)}, u32[]{:S(2)}, u32[]{:S(2)}) async-start(bf16[8,2,3072]{2,1,0:T(2,128)(2,1)} %reshape.1038), calls=%async_computation.5 | async-start | bytes 196608 | tf_op jit(solution)/shard_map/all_to_all | solution.py:82
  314.8 5.4 %all-to-all-done.5 = bf16[8,2,3072]{2,1,0:T(2,128)(2,1)S(1)} async-done(((bf16[8,2,3072]{2,1,0:T(2,128)(2,1)}), bf16[8,2,3072]{2,1,0:T(2,128)(2,1)S(1)}, u32[]{:S(2)}, u32[]{:S(2)}) %all-to-all-start.5) | async-done | bytes 98336 | tf_op jit(solution)/shard_map/all_to_all | solution.py:82
  321.0 3.5 all-to-all-start.6
  324.6 11.6 %all-to-all-done.6 = bf16[1,8,1,16,384]{4,1,2,0,3:T(8,128)(2,1)S(1)} async-done(((bf16[1,8,1,16,384]{4,1,2,0,3:T(8,128)(2,1)}), bf16[1,8,1,16,384]{4,1,2,0,3:T(8,128)(2,1)S(1)}, u32[]{:S(2)}, u32[]{:S(2)}) %all-to-all-start.6) | async-done | bytes 98336 | tf_op jit(solution)/shard_map/all_to_all | solution.py:70
  346.1 4.2 %all-to-all-start.7 = ((bf16[1,8,16,1,384]{4,1,3,0,2:T(8,128)(2,1)}), bf16[1,8,16,1,384]{4,1,3,0,2:T(8,128)(2,1)}, u32[]{:S(2)}, u32[]{:S(2)}) async-start(bf16[1,8,16,1,384]{4,1,3,0,2:T(8,128)(2,1)} %copy.397), calls=%async_computation.7 | async-start | bytes 196608 | tf_op jit(solution)/shard_map/all_to_all | solution.py:74
  350.4 11.6 %all-to-all-done.7 = bf16[1,8,16,1,384]{4,1,3,0,2:T(8,128)(2,1)} async-done(((bf16[1,8,16,1,384]{4,1,3,0,2:T(8,128)(2,1)}), bf16[1,8,16,1,384]{4,1,3,0,2:T(8,128)(2,1)}, u32[]{:S(2)}, u32[]{:S(2)}) %all-to-all-start.7) | async-done | bytes 98336 | tf_op jit(solution)/shard_map/all_to_all | solution.py:74
  362.0 3.3 all-to-all-start.8
  365.4 4.5 %all-to-all-done.8 = bf16[1,8,1,16,384]{4,1,2,0,3:T(8,128)(2,1)S(1)} async-done(((bf16[1,8,1,16,384]{4,1,2,0,3:T(8,128)(2,1)}), bf16[1,8,1,16,384]{4,1,2,0,3:T(8,128)(2,1)S(1)}, u32[]{:S(2)}, u32[]{:S(2)}) %all-to-all-start.8) | async-done | bytes 98336 | tf_op jit(solution)/shard_map/all_to_all | solution.py:62
  374.9 7.0 %all_to_all.121 = bf16[1,32,1,4,384]{4,3,2,0,1:T(4,128)(2,1)S(1)} all-to-all(bf16[1,32,1,4,384]{4,3,2,0,1:T(4,128)(2,1)S(1)} %copy.419), channel_id=1, replica_groups=mesh['gz'=4,'gy'=16,'gx'=8] {'gz'}, dimensions={1} | all-to-all | bytes 196608 | tf_op jit(solution)/shard_map/all_to_all | solution.py:66
  (226 shorter events, 64.7 us)
Async XLA Ops:
  6.5 178.0 %all-gather.2.cloned.1.call-start = ((), (), s32[]{:S(2)}) async-start(), calls=%async_computation.10 | async-start | bytes 3649536 | tf_op jit(solution)/shard_map/all_gather | solution.py:91
  64.5 119.2 %all-to-all-start = ((bf16[1,8,1,16,384]{4,1,2,0,3:T(8,128)(2,1)}), bf16[1,8,1,16,384]{4,1,2,0,3:T(8,128)(2,1)S(1)}, u32[]{:S(2)}, u32[]{:S(2)}) async-start(bf16[1,8,1,16,384]{4,1,2,0,3:T(8,128)(2,1)} %bitcast.315), calls=%async_computation | async-start | bytes 196608 | tf_op jit(solution)/shard_map/all_to_all | solution.py:62
  215.2 9.8 %copy-start.29 = (f32[32,4,6]{0,1,2:T(4,128)}, f32[32,4,6]{0,1,2:T(4,128)S(1)}, u32[]{:S(2)}) copy-start(f32[32,4,6]{0,1,2:T(4,128)S(1)} %fusion.117) | copy-start | bytes 9220
  222.0 2.7 copy-start.14
  223.7 1.3 copy-start.22
  223.7 1.3 copy-start.24
  236.6 19.5 %all-to-all-start.2 = ((bf16[1,8,1,16,384]{4,1,2,0,3:T(8,128)(2,1)}), bf16[1,8,1,16,384]{4,1,2,0,3:T(8,128)(2,1)}, u32[]{:S(2)}, u32[]{:S(2)}) async-start(bf16[1,8,1,16,384]{4,1,2,0,3:T(8,128)(2,1)} %bitcast.343), calls=%async_computation.2 | async-start | bytes 196608 | tf_op jit(solution)/shard_map/all_to_all | solution.py:70
  264.8 2.6 copy-start.16
  265.0 2.7 copy-start.18
  266.3 1.3 copy-start.20
  266.3 1.6 copy-start.6
  269.7 17.9 %all-to-all-start.3 = ((bf16[1,8,16,1,384]{4,1,3,0,2:T(8,128)(2,1)}), bf16[1,8,16,1,384]{4,1,3,0,2:T(8,128)(2,1)S(1)}, u32[]{:S(2)}, u32[]{:S(2)}) async-start(bf16[1,8,16,1,384]{4,1,3,0,2:T(8,128)(2,1)} %copy.362), calls=%async_computation.3 | async-start | bytes 196608 | tf_op jit(solution)/shard_map/all_to_all | solution.py:74
  288.3 13.2 %all-to-all-start.4 = ((bf16[2,8,1,16,384]{4,3,2,0,1:T(8,128)(2,1)}), bf16[2,8,1,16,384]{4,3,2,0,1:T(8,128)(2,1)S(1)}, u32[]{:S(2)}, u32[]{:S(2)}) async-start(bf16[2,8,1,16,384]{4,3,2,0,1:T(8,128)(2,1)} %copy.363), calls=%async_computation.4 | async-start | bytes 393216 | tf_op jit(solution)/shard_map/all_to_all | solution.py:78
  301.5 1.8 copy-start.13
  305.2 1.2 copy-start.4
  306.4 18.1 %copy-start.28 = (f32[8,6,16]{2,1,0:T(8,128)S(1)}, f32[8,6,16]{2,1,0:T(8,128)}, u32[]{:S(2)}) copy-start(f32[8,6,16]{2,1,0:T(8,128)} %copy-done.27) | copy-start | bytes 9220
  306.9 29.7 %copy-start.10 = (f32[8,6,16,16]{2,3,1,0:T(8,128)S(1)}, f32[8,6,16,16]{2,3,1,0:T(8,128)}, u32[]{:S(2)}) copy-start(f32[8,6,16,16]{2,3,1,0:T(8,128)} %copy-done.9) | copy-start | bytes 147460
  309.7 10.6 %all-to-all-start.5 = ((bf16[8,2,3072]{2,1,0:T(2,128)(2,1)}), bf16[8,2,3072]{2,1,0:T(2,128)(2,1)S(1)}, u32[]{:S(2)}, u32[]{:S(2)}) async-start(bf16[8,2,3072]{2,1,0:T(2,128)(2,1)} %reshape.1038), calls=%async_computation.5 | async-start | bytes 196608 | tf_op jit(solution)/shard_map/all_to_all | solution.py:82
  314.8 22.0 %copy-start.17 = (bf16[8,16,6,64]{3,2,1,0:T(8,128)(2,1)S(1)}, bf16[8,16,6,64]{3,2,1,0:T(8,128)(2,1)}, u32[]{:S(2)}) copy-start(bf16[8,16,6,64]{3,2,1,0:T(8,128)(2,1)} %convert_element_type.462) | copy-start | bytes 294916
  321.0 15.2 %all-to-all-start.6 = ((bf16[1,8,1,16,384]{4,1,2,0,3:T(8,128)(2,1)}), bf16[1,8,1,16,384]{4,1,2,0,3:T(8,128)(2,1)S(1)}, u32[]{:S(2)}, u32[]{:S(2)}) async-start(bf16[1,8,1,16,384]{4,1,2,0,3:T(8,128)(2,1)} %copy.376), calls=%async_computation.6 | async-start | bytes 196608 | tf_op jit(solution)/shard_map/all_to_all | solution.py:70
  336.9 1.5 copy-start.19
  338.4 1.3 copy-start.26
  341.2 1.8 copy-start.3
  342.8 7.5 %copy-start.36 = (f32[4,8,4]{1,0,2:T(4,128)S(1)}, f32[4,8,4]{1,0,2:T(4,128)}, u32[]{:S(2)}) copy-start(f32[4,8,4]{1,0,2:T(4,128)} %get-tuple-element.19) | copy-start | bytes 1540
  342.8 22.5 %copy-start.35 = (f32[4,6,32]{2,1,0:T(8,128)S(1)}, f32[4,6,32]{2,1,0:T(8,128)}, u32[]{:S(2)}) copy-start(f32[4,6,32]{2,1,0:T(8,128)} %copy-done.34) | copy-start | bytes 9220
  342.8 22.5 %copy-start.30 = (f32[32,4,6]{0,1,2:T(4,128)S(1)}, f32[32,4,6]{0,1,2:T(4,128)}, u32[]{:S(2)}) copy-start(f32[32,4,6]{0,1,2:T(4,128)} %copy-done.29) | copy-start | bytes 9220
  342.8 22.5 %copy-start.31 = (f32[32,4,6]{0,1,2:T(4,128)S(1)}, f32[32,4,6]{0,1,2:T(4,128)}, u32[]{:S(2)}) copy-start(f32[32,4,6]{0,1,2:T(4,128)} %fusion.118) | copy-start | bytes 9220
  342.8 27.1 %copy-start.5 = (bf16[1,384,384]{2,1,0:T(8,128)(2,1)S(1)}, bf16[1,384,384]{2,1,0:T(8,128)(2,1)}, u32[]{:S(2)}) copy-start(bf16[1,384,384]{2,1,0:T(8,128)(2,1)} %copy.430) | copy-start | bytes 884740
  343.0 27.4 %copy-start.12 = (f32[4,6,32,32]{2,3,1,0:T(8,128)S(1)}, f32[4,6,32,32]{2,3,1,0:T(8,128)}, u32[]{:S(2)}) copy-start(f32[4,6,32,32]{2,3,1,0:T(8,128)} %copy-done.11) | copy-start | bytes 294916
  344.4 26.1 %copy-start.15 = (bf16[32,4,6,64]{3,2,0,1:T(8,128)(2,1)S(1)}, bf16[32,4,6,64]{3,2,0,1:T(8,128)(2,1)}, u32[]{:S(2)}) copy-start(bf16[32,4,6,64]{3,2,0,1:T(8,128)(2,1)} %convert_element_type.449) | copy-start | bytes 294916
  346.1 15.8 %all-to-all-start.7 = ((bf16[1,8,16,1,384]{4,1,3,0,2:T(8,128)(2,1)}), bf16[1,8,16,1,384]{4,1,3,0,2:T(8,128)(2,1)}, u32[]{:S(2)}, u32[]{:S(2)}) async-start(bf16[1,8,16,1,384]{4,1,3,0,2:T(8,128)(2,1)} %copy.397), calls=%async_computation.7 | async-start | bytes 196608 | tf_op jit(solution)/shard_map/all_to_all | solution.py:74
  362.0 7.9 %all-to-all-start.8 = ((bf16[1,8,1,16,384]{4,1,2,0,3:T(8,128)(2,1)}), bf16[1,8,1,16,384]{4,1,2,0,3:T(8,128)(2,1)S(1)}, u32[]{:S(2)}, u32[]{:S(2)}) async-start(bf16[1,8,1,16,384]{4,1,2,0,3:T(8,128)(2,1)} %bitcast.73), calls=%async_computation.8 | async-start | bytes 196608 | tf_op jit(solution)/shard_map/all_to_all | solution.py:62
  (14 other events, 13.2 us)
Sparse Core Ops, SparseCore 0:
  63.1 68.6 all-gather.1
where the time goes:
time: 395 us; the launch traced here: 389 us
  blocking collectives  180 us (46%)
  local copies, waits for them, and re-layouts  71.4 us (18%)
  waiting for transfers between devices  49.2 us (12%)
  starting transfers between devices  40.6 us (10%)
  other arithmetic  17.9 us (5%)
  matrix products  16.1 us (4%)
  between operations  14.5 us (4%)
    all_gather x1, blocking collectives, local(): lax.all_gather(part_outp, ('gz', 'gx'), axis=2, tiled=True)  62.5 us
    all_gather x1, blocking collectives, local(): lax.all_gather(w_project, 'gy', axis=1, tiled=True)  55.6 us
    all_gather x1, blocking collectives, local(): lax.all_gather(w_output, 'gy', axis=1, tiled=True)  47.6 us
    unnamed x87, local copies, waits for them, and re-layouts  27.9 us
    all_to_all x2, waiting for transfers between devices, rows_in(): lax.all_to_all(stacked, 'gy', split_axis=2, concat_axis=3, tiled=True)  22.4 us
    all_to_all x2, waiting for transfers between devices, rows_out(): lax.all_to_all(stacked, 'gy', split_axis=3, concat_axis=2, tiled=True)  16.9 us
    all_to_all x2, blocking collectives, depth_in(): lax.all_to_all(stacked, 'gz', split_axis=1, concat_axis=3, tiled=True)  14.1 us
    slice x2, local copies, waits for them, and re-layouts, column_fn(): return along_columns(member, proj_full[2], outp_full[2])  11.8 us
  transfers between devices with their start and end apart: 9, of which 6 were waited for; matrix products, arithmetic and copies ran while one was open for 6% of the time, Pallas kernels for 0%

commit v1 on v0

v1 whole, which is shorter than its diff:
```python
import functools

import jax
import jax.numpy as jnp
from jax import lax
from jax.experimental import pallas as pl
from jax.experimental.pallas import tpu as pltpu
from jax.sharding import PartitionSpec as P

MESH = pl.DeviceIdType.MESH
F32 = jnp.float32
BF16 = jnp.bfloat16
HEADS = 6
HEAD = 64
D = 384
EPS = 1e-06
TOK = 128
NZ, NY, NX = 4, 16, 8
NG = NZ * NX
QKV = 36
OUT = 12
CH = QKV + OUT
ROWS = 24


def dot(a, b, ca, cb):
    return lax.dot_general(a, b, (((ca,), (cb,)), ((), ())), preferred_element_type=F32)


def roll4(x):
    return pltpu.roll(x, 4, x.ndim - 2)


def low_half(shape):
    return lax.broadcasted_iota(jnp.int32, shape, len(shape) - 2) % 8 < 4


def swap_halves(u, v):
    low = low_half(u.shape)
    return jnp.where(low, u, roll4(v)), jnp.where(low, roll4(u), v)


def forward(stream, w_t, wo_t, mask, save):
    inv = lax.rsqrt(jnp.mean(stream * stream, axis=-1, keepdims=True) + EPS)
    normed = (stream * inv).astype(BF16)
    packed = dot(w_t, normed, 1, 1)
    heads = packed.reshape(3, HEADS, HEAD, TOK)
    inv_qk = lax.rsqrt(jnp.mean(heads[:2] * heads[:2], axis=2, keepdims=True) + EPS)
    qk = (heads[:2] * inv_qk).astype(BF16)
    val = heads[2].astype(BF16)
    mixed = []
    for h in range(HEADS):
        scores = dot(qk[1, h], qk[0, h], 0, 0) * (HEAD**-0.5)
        powers = jnp.exp(scores)
        if mask is not None:
            powers = jnp.where(mask, powers, 0.0)
        attn = (powers / jnp.sum(powers, axis=0, keepdims=True)).astype(BF16)
        save["attn"][h] = attn
        mixed.append(dot(val[h], attn, 1, 0).astype(BF16))
    mixed = jnp.concatenate(mixed, axis=0)
    save["inv"][...] = inv
    save["normed"][...] = normed
    save["inv_qk"][...] = inv_qk.reshape(2 * HEADS, 1, TOK)
    save["qkv"][: 2 * HEADS] = qk.reshape(2 * HEADS, HEAD, TOK)
    save["qkv"][2 * HEADS :] = val
    if wo_t is None:
        return None
    return stream + dot(wo_t, mixed, 1, 0).T


def backward(grad, w_t, wo_t, save):
    mixed_grad = dot(grad, wo_t, 1, 0).T.astype(BF16)
    packed_grad = [None] * (3 * HEADS)
    for h in range(HEADS):
        q, k, v = save["qkv"][h], save["qkv"][HEADS + h], save["qkv"][2 * HEADS + h]
        attn = save["attn"][h]
        attn32 = attn.astype(F32)
        d_mixed = mixed_grad[h * HEAD : (h + 1) * HEAD]
        d_attn = dot(v, d_mixed, 0, 0)
        d_v = dot(d_mixed, attn, 1, 1)
        d_scores = attn32 * (d_attn - jnp.sum(d_attn * attn32, axis=0, keepdims=True))
        d_scores = (d_scores * (HEAD**-0.5)).astype(BF16)
        d_q = dot(k, d_scores, 1, 0)
        d_k = dot(q, d_scores, 1, 1)
        for at, unit, d_unit in ((h, q, d_q), (HEADS + h, k, d_k)):
            unit32 = unit.astype(F32)
            proj = jnp.mean(d_unit * unit32, axis=0, keepdims=True)
            packed_grad[at] = (save["inv_qk"][at] * (d_unit - unit32 * proj)).astype(BF16)
        packed_grad[2 * HEADS + h] = d_v.astype(BF16)
    packed_grad = jnp.concatenate(packed_grad, axis=0)
    d_normed = dot(packed_grad, w_t, 0, 0)
    normed32 = save["normed"][...].astype(F32)
    proj = jnp.mean(d_normed * normed32, axis=-1, keepdims=True)
    return grad.astype(F32) + save["inv"][...] * (d_normed - normed32 * proj)


def line_mask(lines):
    row = lax.broadcasted_iota(jnp.int32, (TOK, TOK), 0)
    col = lax.broadcasted_iota(jnp.int32, (TOK, TOK), 1)
    return row % lines == col % lines


def split_home(block, out):
    x = block.astype(F32).reshape(4, 2, 2, 8, D)
    for half in range(2):
        low, high = swap_halves(x[:, 0, half], x[:, 1, half])
        out[2 * half] = low.reshape(32, D).astype(BF16)
        out[2 * half + 1] = high.reshape(32, D).astype(BF16)


def join_home(got, out):
    for half in range(2):
        u = got[2 * half].astype(F32).reshape(4, 8, D)
        v = got[2 * half + 1].astype(F32).reshape(4, 8, D)
        low, high = swap_halves(u, v)
        for m in range(4):
            out[2 * m, 8 * half : 8 * half + 8] = low[m].astype(BF16)
            out[2 * m + 1, 8 * half : 8 * half + 8] = high[m].astype(BF16)


def pack8(x, out):
    x = x.reshape(NY, 8, D)
    out[:, 0:16] = jnp.concatenate([x[:, :, 0:128], x[:, :, 128:256]], axis=1).astype(BF16)
    out[:, 16:32] = jnp.concatenate([x[:, :, 256:384], x[:, :, 256:384]], axis=1).astype(BF16)


def unpack8(got):
    x = got[...].astype(F32)
    return jnp.concatenate([x[:, 0:8], x[:, 8:16], x[:, 16:24]], axis=2).reshape(TOK, D)


def pack4(x, out):
    x = x.reshape(16, 8, D)
    first, second, third = x[:, :, 0:128], x[:, :, 128:256], x[:, :, 256:384]
    low, high = swap_halves(first, second)
    out[:, 0] = jnp.concatenate([low, third], axis=1).astype(BF16)
    out[:, 1] = jnp.concatenate([high, roll4(third)], axis=1).astype(BF16)


def unpack4(got):
    even, odd = got[:, 0].astype(F32), got[:, 1].astype(F32)
    first, second = swap_halves(even[:, 0:8], odd[:, 0:8])
    third = swap_halves(even[:, 8:16], odd[:, 8:16])[0]
    return jnp.concatenate([first, second, third], axis=2).reshape(TOK, D)


def own_chunk(w_ref, wo_ref, stage):
    rows = 3 * ROWS
    eye = (
        lax.broadcasted_iota(jnp.int32, (rows, 128), 0) == lax.broadcasted_iota(jnp.int32, (rows, 128), 1)
    ).astype(BF16)
    stage[0:QKV] = dot(w_ref[...], eye, 0, 0)
    stage[QKV:CH] = dot(wo_ref[...], eye, 0, 0)
    return stage[...].astype(BF16)


def join_features(parts, layer):
    lane = lax.broadcasted_iota(jnp.int32, (CH, 128), 1)
    tiles = []
    for t in range(3):
        tile = None
        for g in range(NY):
            start = ROWS * g - 128 * t
            if start + ROWS <= 0 or start >= 128:
                continue
            piece = pltpu.roll(parts[g], (start - ROWS * layer) % 128, 1)
            tile = piece if tile is None else jnp.where(lane >= start, piece, tile)
        tiles.append(tile)
    return jnp.concatenate(tiles, axis=1)


def slot_of(unit):
    return (unit % 2) * 16 + (unit // 8) * 4 + (unit % 8) // 2


def compact(gathered, layer, w_t, wo_t, stage):
    for unit in range(NG):
        chunk = gathered[layer, slot_of(unit)].astype(F32)
        stage[QKV * unit : QKV * (unit + 1)] = chunk[:QKV]
        stage[3 * D + OUT * unit : 3 * D + OUT * (unit + 1)] = chunk[QKV:]
    w_t[layer] = stage[: 3 * D].astype(BF16)
    wo_t[layer] = stage[3 * D :].astype(BF16)


def kernel(
    vol, cot, w_in, wo_in, out,
    h1s, h1r, h2s, h2r, h3s, h3r, g3s, g3r, g2s, g2r, g1s, g1r, cotr,
    wsend, wparts, gathered, w_t, wo_t, wstage, cstage,
    *rest,
):
    saves = []
    for i in range(3):
        a, b, c, d, e = rest[5 * i : 5 * i + 5]
        saves.append(dict(attn=a, inv=b, normed=c, inv_qk=d, qkv=e))
    a2a_send, a2a_recv, cot_send, cot_recv, w_sems, wy_send, wy_recv, wx_send, wx_recv, wc_send, wc_recv = rest[15:]
    gz, gy, gx = lax.axis_index("gz"), lax.axis_index("gy"), lax.axis_index("gx")
    core, ylo = gx % 2, gx // 2
    line = ((gz + NZ - 1) % NZ) * NX + gx
    column = gx * NZ + gz

    def line_owner(d):
        return (d // NX + 1) % NZ, d % NX

    def column_owner(s):
        return s % NZ, s // NZ

    def send(src, dst, ssem, rsem, to):
        pltpu.make_async_remote_copy(
            src_ref=src, dst_ref=dst, send_sem=ssem, recv_sem=rsem, device_id=to, device_id_type=MESH
        ).start()

    def drain(ref, sem):
        pltpu.make_async_copy(ref, ref, sem).wait()

    def each(count, body):
        lax.fori_loop(0, count, lambda k, c: (body(k), c)[1], 0)

    barrier = pltpu.get_barrier_semaphore()

    def greet(to):
        pl.semaphore_signal(barrier, inc=1, device_id=to, device_id_type=MESH)

    each(NY - 1, lambda k: greet((gz, (gy + 1 + k) % NY, gx)))

    def greet_line(k):
        s = (column + 1 + k) % NG
        z, x = column_owner(s)
        greet((z, gy, x))

    each(NG - 1, greet_line)
    each(NX, lambda k: greet((gy // 4, line // 2, k)))

    wsend[...] = own_chunk(w_in, wo_in, cstage)
    split_home(vol[...], h1s)
    pl.semaphore_wait(barrier, NY - 1 + NG - 1 + 8)

    each(
        NY - 1,
        lambda k: send(wsend, wparts.at[gy], w_sems.at[0], w_sems.at[1], (gz, (gy + 1 + k) % NY, gx)),
    )
    pltpu.make_async_copy(wsend, wparts.at[gy], w_sems.at[1]).start()

    def gz_exchange(src, dst, n):
        def body(k):
            to = (gz + 1 + k) % NZ
            send(src.at[to], dst.at[gz], a2a_send.at[n], a2a_recv.at[n], (to, gy, gx))

        each(NZ - 1, body)
        pltpu.make_async_copy(src.at[gz], dst.at[gz], a2a_recv.at[n]).start()

    def gy_exchange(src, dst, n):
        def body(k):
            to = (gy + 1 + k) % NY
            send(src.at[to], dst.at[gy], a2a_send.at[n], a2a_recv.at[n], (gz, to, gx))

        each(NY - 1, body)
        pltpu.make_async_copy(src.at[gy], dst.at[gy], a2a_recv.at[n]).start()

    gz_exchange(h1s, h1r, 0)

    def send_cot(k):
        z, x = line_owner(2 * gy + k % 2)
        send(cot.at[k], cotr.at[gx], cot_send, cot_recv, (z, 4 * gz + k // 2, x))

    each(8, send_cot)

    drain(wparts, w_sems.at[1])
    parts = wparts[...].astype(F32)
    own = gz * 4 + ylo
    for layer in range(3):
        gathered[layer, core * 16 + own] = join_features(parts, layer).astype(BF16)

        def send_y(k, layer=layer):
            to = (ylo + 1 + k) % 4
            block = gathered.at[layer, core * 16 + own]
            send(block, block, wy_send.at[layer], wy_recv.at[layer], (gz, gy, to * 2 + core))

        each(3, send_y)

    def run4(layer, c, z):
        return gathered.at[layer, pl.ds(c * 16 + z * 4, 4)]

    for layer in range(3):
        drain(gathered.at[layer, pl.ds(0, 3)], wy_recv.at[layer])
        mine = run4(layer, core, gz)

        def send_x(k, layer=layer, mine=mine):
            to = (gz + 1 + k) % NZ
            send(mine, mine, wx_send.at[layer], wx_recv.at[layer, gz], (to, gy, gx))

        each(3, send_x)
        send(mine, mine, wc_send.at[layer], wc_recv.at[layer], (gz, gy, gx + 1 - 2 * core))

    def finish_weights(layer):
        def forward_x(k):
            z = (gz + 1 + k) % NZ
            block = run4(layer, core, z)
            drain(block, wx_recv.at[layer, z])
            send(block, block, wc_send.at[layer], wc_recv.at[layer], (gz, gy, gx + 1 - 2 * core))

        each(3, forward_x)
        drain(gathered.at[layer, pl.ds(0, 16)], wc_recv.at[layer])
        compact(gathered, layer, w_t, wo_t, wstage)

    finish_weights(0)
    drain(h1r, a2a_recv.at[0])
    depth_mask = line_mask(4)
    x = h1r[...].reshape(TOK, D).astype(F32)
    x = forward(x, w_t[0], wo_t[0], depth_mask, saves[0])
    pack8(x, h2s)
    gy_exchange(h2s, h2r, 1)

    finish_weights(1)
    drain(h2r, a2a_recv.at[1])
    row_mask = line_mask(8)
    x = forward(unpack8(h2r), w_t[1], wo_t[1], row_mask, saves[1])
    pack4(x, h3s)

    def line_exchange(src, dst, n):
        def body(k):
            d = (line + 1 + k) % NG
            z, x = line_owner(d)
            send(src.at[d // 2, d % 2], dst.at[column // 2, column % 2], a2a_send.at[n], a2a_recv.at[n], (z, gy, x))

        each(NG - 1, body)
        pltpu.make_async_copy(
            src.at[line // 2, line % 2], dst.at[column // 2, column % 2], a2a_recv.at[n]
        ).start()

    def column_exchange(src, dst, n):
        def body(k):
            s = (column + 1 + k) % NG
            z, x = column_owner(s)
            send(src.at[s // 2, s % 2], dst.at[line // 2, line % 2], a2a_send.at[n], a2a_recv.at[n], (z, gy, x))

        each(NG - 1, body)
        pltpu.make_async_copy(
            src.at[column // 2, column % 2], dst.at[line // 2, line % 2], a2a_recv.at[n]
        ).start()

    line_exchange(h3s, h3r, 2)

    finish_weights(2)
    drain(cotr, cot_recv)
    drain(h3r, a2a_recv.at[2])
    forward(unpack4(h3r), w_t[2], None, None, saves[2])
    g = backward(cotr[...].reshape(TOK, D), w_t[2], wo_t[2], saves[2])
    pack4(g, g3s)
    column_exchange(g3s, g3r, 3)

    drain(g3r, a2a_recv.at[3])
    g = backward(unpack4(g3r).astype(BF16), w_t[1], wo_t[1], saves[1])
    pack8(g, g2s)
    gy_exchange(g2s, g2r, 4)

    drain(g2r, a2a_recv.at[4])
    g = backward(unpack8(g2r).astype(BF16), w_t[0], wo_t[0], saves[0])
    g1s[...] = g.astype(BF16).reshape(NZ, 32, D)
    gz_exchange(g1s, g1r, 5)

    drain(wparts.at[pl.ds(0, NY - 1)], w_sems.at[0])
    drain(h1r.at[pl.ds(0, NZ - 1)], a2a_send.at[0])
    drain(cotr, cot_send)
    for layer in range(3):
        drain(gathered.at[layer, pl.ds(0, 3)], wy_send.at[layer])
        drain(gathered.at[layer, pl.ds(0, 12)], wx_send.at[layer])
        drain(gathered.at[layer, pl.ds(0, 16)], wc_send.at[layer])
    for n, ref in ((1, h2r), (4, g2r)):
        drain(ref.at[pl.ds(0, NY - 1)], a2a_send.at[n])
    for n, ref in ((2, h3r), (3, g3r)):
        drain(ref.at[pl.ds(0, 15)], a2a_send.at[n])
        drain(ref.at[15, pl.ds(0, 1)], a2a_send.at[n])
    drain(g1r.at[pl.ds(0, NZ - 1)], a2a_send.at[5])

    drain(g1r, a2a_recv.at[5])
    join_home(g1r, out)


def local(volume, cotangent, w_project, w_output):
    vmem = pltpu.VMEM
    save = [
        vmem((HEADS, TOK, TOK), BF16),
        vmem((TOK, 1), F32),
        vmem((TOK, D), BF16),
        vmem((2 * HEADS, 1, TOK), F32),
        vmem((3 * HEADS, HEAD, TOK), BF16),
    ]
    dma = pltpu.SemaphoreType.DMA
    scratch = [
        *[vmem((NZ, 32, D), BF16)] * 2,
        *[vmem((NY, 32, 128), BF16)] * 2,
        *[vmem((16, 2, 16, 128), BF16)] * 4,
        *[vmem((NY, 32, 128), BF16)] * 2,
        *[vmem((NZ, 32, D), BF16)] * 2,
        vmem((NX, 16, D), BF16),
        vmem((CH, 128), BF16),
        vmem((NY, CH, 128), BF16),
        vmem((3, NG, CH, D), BF16),
        vmem((3, 3 * D, D), BF16),
        vmem((3, D, D), BF16),
        vmem((4 * D, D), F32),
        vmem((CH, 128), F32),
        *save * 3,
        dma((6,)),
        dma((6,)),
        dma,
        dma,
        dma((2,)),
        dma((3,)),
        dma((3,)),
        dma((3,)),
        dma((3, NZ)),
        dma((3,)),
        dma((3,)),
    ]
    block = volume.shape
    whole = pl.BlockSpec(memory_space=pltpu.VMEM)
    got = pl.pallas_call(
        kernel,
        out_shape=jax.ShapeDtypeStruct((8, 16, D), BF16),
        in_specs=[whole] * 4,
        out_specs=whole,
        scratch_shapes=scratch,
        compiler_params=pltpu.CompilerParams(
            collective_id=0, has_side_effects=True, vmem_limit_bytes=48 * 1024 * 1024
        ),
    )(
        volume.reshape(8, 16, D),
        cotangent.reshape(8, 16, D),
        w_project.reshape(3 * ROWS, QKV),
        w_output.reshape(3 * ROWS, OUT),
    )
    return got.reshape(block)


def solution(mesh):
    return jax.shard_map(
        local,
        mesh=mesh,
        in_specs=(
            P("gz", "gy", "gx", None),
            P("gz", "gy", "gx", None),
            P(None, "gy", ("gz", "gx")),
            P(None, "gy", ("gz", "gx")),
        ),
        out_specs=P("gz", "gy", "gx", None),
        check_vma=False,
    )
```

time: 395 us -> 91 us (0.23); the launches traced: 389 us -> 90.8 us
  blocking collectives: 180 us -> 0 us
  Pallas kernels: 0 us -> 87.5 us
  local copies, waits for them, and re-layouts: 71.4 us -> 3.24 us
  waiting for transfers between devices: 49.2 us -> 0 us
  starting transfers between devices: 40.6 us -> 0 us
  other arithmetic: 17.9 us -> 0 us
  matrix products: 16.1 us -> 0 us
  between operations: 14.5 us -> 0.02 us
    all_gather x3 -> x0, blocking collectives: 166 us -> none  [the longest x1 62.5 us: local(): lax.all_gather(part_outp, ('gz', 'gx'), axis=2, tiled=True)]
    pallas_call x0 -> x1, Pallas kernels: none -> 87.5 us  [local(): pl.pallas_call(kernel, out_shape=jax.ShapeDtypeStruct((8, 16, D), BF16),...]
    all_to_all x8 -> x0, waiting for transfers between devices: 49.2 us -> none  [the longest x2 22.4 us: rows_in(): lax.all_to_all(stacked, 'gy', split_axis=2, concat_axis=3, tiled=True)]
    all_to_all x8 -> x0, starting transfers between devices: 40.6 us -> none  [the longest x2 11.2 us: rows_out(): lax.all_to_all(stacked, 'gy', split_axis=3, concat_axis=2, tiled=True)]
    unnamed x87 -> x8, local copies, waits for them, and re-layouts: 27.9 us -> 3.24 us
    dot_general x28 -> x0, matrix products: 16.1 us -> none  [the longest x6 7.15 us: sublayer(): packed = jnp.dot(normed, w_inner, preferred_element_type=jnp.float32)]
    slice x11 -> x0, local copies, waits for them, and re-layouts: 14.3 us -> none  [the longest x2 11.8 us: column_fn(): return along_columns(member, proj_full[2], outp_full[2])]
    all_to_all x2 -> x0, blocking collectives: 14.1 us -> none  [depth_in(): lax.all_to_all(stacked, 'gz', split_axis=1, concat_axis=3, tiled=True)]
  transfers between devices with their start and end apart: 9 -> 0, of which waited for: 6 -> 0; matrix products, arithmetic and copies ran while one was open for 6% -> 0% of each run, Pallas kernels for 0% -> 0%
where the time goes in v1:
time: 91 us; the launch traced here: 90.8 us
  Pallas kernels  87.5 us (96%)
  local copies, waits for them, and re-layouts  3.24 us (4%)
    pallas_call x1, Pallas kernels, local(): pl.pallas_call(kernel, out_shape=jax.ShapeDtypeStruct((8, 16, D), BF16),...  87.5 us
    unnamed x8, local copies, waits for them, and re-layouts  3.24 us

profile of v1, /device:TPU:1, one launch (start us, length us, event | category | flops | bytes accessed | tf_op | source)
XLA Modules:
  0.0 90.8 jit_solution(7594259989091143404)
XLA Ops:
  0.0 0.0 copy-start.2
  0.0 0.8 copy.5
  0.8 0.0 copy-done.2
  0.8 0.0 copy-start
  0.8 0.9 copy-done
  1.7 0.0 copy-start.1
  1.7 0.9 copy-done.1
  2.6 87.5 %shard_map.46 = bf16[8,16,384]{2,1,0:T(8,128)(2,1)S(1)} custom-call(bf16[8,16,384]{2,1,0:T(8,128)(2,1)S(1)} %bitcast.8, bf16[8,16,384]{2,1,0:T(8,128)(2,1)S(1)} %bitcast.9, bf16[72,36]{1,0:T(8,128)(2,1)S(1)} %bitcast.11, bf16[72,12]{1,0:T(8,128)(2,1)S(1)} %bitcast.10), custom_call_target="tpu_custom_call" | custom-call | tf_op jit(solution)/shard_map/pallas_call | solution.py:418
  90.1 0.6 copy.8
Async XLA Ops:
  0.0 0.8 copy-start.2
  0.8 0.9 copy-start
  1.7 0.9 copy-start.1

commit v2 on v1

--- a/solution.py
+++ b/solution.py
@@ -148,9 +148,10 @@
     rows = 3 * ROWS
     eye = (
         lax.broadcasted_iota(jnp.int32, (rows, 128), 0) == lax.broadcasted_iota(jnp.int32, (rows, 128), 1)
-    ).astype(BF16)
-    stage[0:QKV] = dot(w_ref[...], eye, 0, 0)
-    stage[QKV:CH] = dot(wo_ref[...], eye, 0, 0)
+    ).astype(F32)
+    block = jnp.concatenate([w_ref[i].astype(F32) for i in range(3)], axis=0).astype(BF16)
+    stage[0:QKV] = dot(block, eye.astype(BF16), 0, 0)
+    stage[QKV:CH] = sum(dot(wo_ref[i], eye[ROWS * i : ROWS * (i + 1)].astype(BF16), 1, 0) for i in range(3))
     return stage[...].astype(BF16)
 
 
@@ -183,21 +184,29 @@
 
 
 def kernel(
-    vol, cot, w_in, wo_in, out,
+    vol_hbm, cot_hbm, w_hbm, wo_hbm, out,
+    vol, w_in, wo_in,
     h1s, h1r, h2s, h2r, h3s, h3r, g3s, g3r, g2s, g2r, g1s, g1r, cotr,
-    wsend, wparts, gathered, w_t, wo_t, wstage, cstage,
+    wparts, gathered, w_t, wo_t, wstage, cstage,
     *rest,
 ):
     saves = []
     for i in range(3):
         a, b, c, d, e = rest[5 * i : 5 * i + 5]
         saves.append(dict(attn=a, inv=b, normed=c, inv_qk=d, qkv=e))
-    a2a_send, a2a_recv, cot_send, cot_recv, w_sems, wy_send, wy_recv, wx_send, wx_recv, wc_send, wc_recv = rest[15:]
+    load_sems, a2a_send, a2a_recv, cot_send, cot_recv, w_sems, wd_send, wd_recv, wx_recv, wc_send, wc_recv = rest[15:]
     gz, gy, gx = lax.axis_index("gz"), lax.axis_index("gy"), lax.axis_index("gx")
     core, ylo = gx % 2, gx // 2
     line = ((gz + NZ - 1) % NZ) * NX + gx
     column = gx * NZ + gz
 
+    loads = [
+        pltpu.make_async_copy(src, dst, load_sems.at[i])
+        for i, (src, dst) in enumerate(((w_hbm, w_in), (wo_hbm, wo_in), (vol_hbm, vol)))
+    ]
+    for load in loads:
+        load.start()
+
     def line_owner(d):
         return (d // NX + 1) % NZ, d % NX
 
@@ -230,15 +239,17 @@
     each(NG - 1, greet_line)
     each(NX, lambda k: greet((gy // 4, line // 2, k)))
 
-    wsend[...] = own_chunk(w_in, wo_in, cstage)
-    split_home(vol[...], h1s)
+    loads[0].wait()
+    loads[1].wait()
+    wparts[gy] = own_chunk(w_in, wo_in, cstage)
     pl.semaphore_wait(barrier, NY - 1 + NG - 1 + 8)
 
     each(
         NY - 1,
-        lambda k: send(wsend, wparts.at[gy], w_sems.at[0], w_sems.at[1], (gz, (gy + 1 + k) % NY, gx)),
+        lambda k: send(
+            wparts.at[gy], wparts.at[gy], w_sems.at[0], w_sems.at[1], (gz, (gy + 1 + k) % NY, gx)
+        ),
     )
-    pltpu.make_async_copy(wsend, wparts.at[gy], w_sems.at[1]).start()
 
     def gz_exchange(src, dst, n):
         def body(k):
@@ -256,51 +267,91 @@
         each(NY - 1, body)
         pltpu.make_async_copy(src.at[gy], dst.at[gy], a2a_recv.at[n]).start()
 
+    loads[2].wait()
+    split_home(vol[...], h1s)
     gz_exchange(h1s, h1r, 0)
+
+    drain(wparts.at[pl.ds(0, NY - 1)], w_sems.at[1])
+    parts = wparts[...].astype(F32)
+    own = gz * 4 + ylo
+    sibling = (gz, gy, gx + 1 - 2 * core)
+
+    def piece(layer, at):
+        return gathered.at[layer, core * 16 + at]
+
+    def run4(layer, z):
+        return gathered.at[layer, pl.ds(core * 16 + z * 4, 4)]
+
+    def send_y(layer):
+        def body(k):
+            to = (ylo + 1 + k) % 4
+            block = piece(layer, own)
+            send(block, block, wd_send.at[layer], wd_recv.at[layer, own], (gz, gy, to * 2 + core))
+
+        each(3, body)
+
+    def send_x(layer, block, sem):
+        each(3, lambda k: send(block, block, wd_send.at[layer], sem, ((gz + 1 + k) % NZ, gy, gx)))
+
+    def send_core(layer, block):
+        send(block, block, wc_send.at[layer], wc_recv.at[layer], sibling)
+
+    gathered[0, core * 16 + own] = join_features(parts, 0).astype(BF16)
+    send_y(0)
+    send_x(0, piece(0, own), wd_recv.at[0, own])
+    send_core(0, piece(0, own))
+    for layer in (1, 2):
+        gathered[layer, core * 16 + own] = join_features(parts, layer).astype(BF16)
+
+    def pass_y(k):
+        at = gz * 4 + (ylo + 1 + k) % 4
+        block = piece(0, at)
+        drain(block, wd_recv.at[0, at])
+        send_x(0, block, wd_recv.at[0, at])
+        send_core(0, block)
+
+    each(3, pass_y)
+    send_y(1)
+    send_y(2)
+
+    def pass_x(k):
+        at = ((gz + 1 + k % 3) % NZ) * 4 + (ylo + k // 3) % 4
+        block = piece(0, at)
+        drain(block, wd_recv.at[0, at])
+        send_core(0, block)
+
+    each(12, pass_x)
+
+    def spread(layer):
+        def wait_y(k):
+            at = gz * 4 + (ylo + 1 + k) % 4
+            drain(piece(layer, at), wd_recv.at[layer, at])
+
+        each(3, wait_y)
+        block = run4(layer, gz)
+        send_x(layer, block, wx_recv.at[layer, gz])
+        send_core(layer, block)
+
+    def pass_runs(layer):
+        def body(k):
+            z = (gz + 1 + k) % NZ
+            block = run4(layer, z)
+            drain(block, wx_recv.at[layer, z])
+            send_core(layer, block)
+
+        each(3, body)
+
+    def finish_weights(layer):
+        drain(gathered.at[layer, pl.ds(0, 16)], wc_recv.at[layer])
+        compact(gathered, layer, w_t, wo_t, wstage)
+
+    spread(1)
 
     def send_cot(k):
         z, x = line_owner(2 * gy + k % 2)
-        send(cot.at[k], cotr.at[gx], cot_send, cot_recv, (z, 4 * gz + k // 2, x))
+        send(cot_hbm.at[k], cotr.at[gx], cot_send, cot_recv, (z, 4 * gz + k // 2, x))
 
     each(8, send_cot)
-
-    drain(wparts, w_sems.at[1])
-    parts = wparts[...].astype(F32)
-    own = gz * 4 + ylo
-    for layer in range(3):
-        gathered[layer, core * 16 + own] = join_features(parts, layer).astype(BF16)
-
-        def send_y(k, layer=layer):
-            to = (ylo + 1 + k) % 4
-            block = gathered.at[layer, core * 16 + own]
-            send(block, block, wy_send.at[layer], wy_recv.at[layer], (gz, gy, to * 2 + core))
-
-        each(3, send_y)
-
-    def run4(layer, c, z):
-        return gathered.at[layer, pl.ds(c * 16 + z * 4, 4)]
-
-    for layer in range(3):
-        drain(gathered.at[layer, pl.ds(0, 3)], wy_recv.at[layer])
-        mine = run4(layer, core, gz)
-
-        def send_x(k, layer=layer, mine=mine):
-            to = (gz + 1 + k) % NZ
-            send(mine, mine, wx_send.at[layer], wx_recv.at[layer, gz], (to, gy, gx))
-
-        each(3, send_x)
-        send(mine, mine, wc_send.at[layer], wc_recv.at[layer], (gz, gy, gx + 1 - 2 * core))
-
-    def finish_weights(layer):
-        def forward_x(k):
-            z = (gz + 1 + k) % NZ
-            block = run4(layer, core, z)
-            drain(block, wx_recv.at[layer, z])
-            send(block, block, wc_send.at[layer], wc_recv.at[layer], (gz, gy, gx + 1 - 2 * core))
-
-        each(3, forward_x)
-        drain(gathered.at[layer, pl.ds(0, 16)], wc_recv.at[layer])
-        compact(gathered, layer, w_t, wo_t, wstage)
 
     finish_weights(0)
     drain(h1r, a2a_recv.at[0])
@@ -310,6 +361,8 @@
     pack8(x, h2s)
     gy_exchange(h2s, h2r, 1)
 
+    spread(2)
+    pass_runs(1)
     finish_weights(1)
     drain(h2r, a2a_recv.at[1])
     row_mask = line_mask(8)
@@ -340,6 +393,7 @@
 
     line_exchange(h3s, h3r, 2)
 
+    pass_runs(2)
     finish_weights(2)
     drain(cotr, cot_recv)
     drain(h3r, a2a_recv.at[2])
@@ -362,8 +416,7 @@
     drain(h1r.at[pl.ds(0, NZ - 1)], a2a_send.at[0])
     drain(cotr, cot_send)
     for layer in range(3):
-        drain(gathered.at[layer, pl.ds(0, 3)], wy_send.at[layer])
-        drain(gathered.at[layer, pl.ds(0, 12)], wx_send.at[layer])
+        drain(gathered.at[layer, pl.ds(0, 15)], wd_send.at[layer])
         drain(gathered.at[layer, pl.ds(0, 16)], wc_send.at[layer])
     for n, ref in ((1, h2r), (4, g2r)):
         drain(ref.at[pl.ds(0, NY - 1)], a2a_send.at[n])
@@ -387,13 +440,15 @@
     ]
     dma = pltpu.SemaphoreType.DMA
     scratch = [
+        vmem((8, 16, D), BF16),
+        vmem((3, ROWS, QKV), BF16),
+        vmem((3, OUT, ROWS), BF16),
         *[vmem((NZ, 32, D), BF16)] * 2,
         *[vmem((NY, 32, 128), BF16)] * 2,
         *[vmem((16, 2, 16, 128), BF16)] * 4,
         *[vmem((NY, 32, 128), BF16)] * 2,
         *[vmem((NZ, 32, D), BF16)] * 2,
         vmem((NX, 16, D), BF16),
-        vmem((CH, 128), BF16),
         vmem((NY, CH, 128), BF16),
         vmem((3, NG, CH, D), BF16),
         vmem((3, 3 * D, D), BF16),
@@ -401,14 +456,14 @@
         vmem((4 * D, D), F32),
         vmem((CH, 128), F32),
         *save * 3,
+        dma((3,)),
         dma((6,)),
         dma((6,)),
         dma,
         dma,
         dma((2,)),
         dma((3,)),
-        dma((3,)),
-        dma((3,)),
+        dma((3, 16)),
         dma((3, NZ)),
         dma((3,)),
         dma((3,)),
@@ -418,17 +473,17 @@
     got = pl.pallas_call(
         kernel,
         out_shape=jax.ShapeDtypeStruct((8, 16, D), BF16),
-        in_specs=[whole] * 4,
+        in_specs=[pl.BlockSpec(memory_space=pltpu.HBM)] * 4,
         out_specs=whole,
         scratch_shapes=scratch,
         compiler_params=pltpu.CompilerParams(
-            collective_id=0, has_side_effects=True, vmem_limit_bytes=48 * 1024 * 1024
+            collective_id=0, has_side_effects=True, vmem_limit_bytes=63_400_000
         ),
     )(
         volume.reshape(8, 16, D),
         cotangent.reshape(8, 16, D),
-        w_project.reshape(3 * ROWS, QKV),
-        w_output.reshape(3 * ROWS, OUT),
+        w_project,
+        jnp.swapaxes(w_output, 1, 2),
     )
     return got.reshape(block)
 

time: 91 us -> 85.4 us (0.938); the launches traced: 90.8 us -> 83.7 us
  Pallas kernels: 87.5 us -> 82.2 us
  local copies, waits for them, and re-layouts: 3.24 us -> 1.54 us
    pallas_call x1, Pallas kernels: 87.5 us -> 82.2 us  [local(): pl.pallas_call(kernel, out_shape=jax.ShapeDtypeStruct((8, 16, D), BF16),...]
    unnamed x8 -> x1, local copies, waits for them, and re-layouts: 3.24 us -> 1.54 us
where the time goes in v2:
time: 85.4 us; the launch traced here: 83.7 us
  Pallas kernels  82.2 us (96%)
  local copies, waits for them, and re-layouts  1.54 us (2%)
    pallas_call x1, Pallas kernels, local(): pl.pallas_call(kernel, out_shape=jax.ShapeDtypeStruct((8, 16, D), BF16),...  82.2 us

profile of v2, /device:TPU:1, one launch (start us, length us, event | category | flops | bytes accessed | tf_op | source)
XLA Modules:
  0.0 83.7 jit_solution(16862554665265280733)
XLA Ops:
  0.0 82.2 %shard_map.46 = bf16[8,16,384]{2,1,0:T(8,128)(2,1)} custom-call(bf16[8,16,384]{2,1,0:T(8,128)(2,1)} %bitcast.7, bf16[8,16,384]{2,1,0:T(8,128)(2,1)} %bitcast.8, bf16[3,24,36]{2,1,0:T(8,128)(2,1)} %w_hbm.1, bf16[3,12,24]{2,1,0:T(8,128)(2,1)} %bitcast.9), custom_call_target="tpu_custom_call" | custom-call | tf_op jit(solution)/shard_map/pallas_call | solution.py:473
  82.2 1.5 %copy.7 = bf16[8,1,16,384]{3,2,1,0:T(8,128)(2,1)} copy(bf16[8,1,16,384]{3,2,1,0:T(8,128)(2,1)} %bitcast.6) | data formatting | bytes 196608

commit v3 on v2

--- a/solution.py
+++ b/solution.py
@@ -38,6 +38,28 @@
 def swap_halves(u, v):
     low = low_half(u.shape)
     return jnp.where(low, u, roll4(v)), jnp.where(low, roll4(u), v)
+
+
+def place(block):
+    return (block % 2) * 8 + block // 2
+
+
+def order_matrix():
+    row = lax.broadcasted_iota(jnp.int32, (D, D), 0)
+    col = lax.broadcasted_iota(jnp.int32, (D, D), 1)
+    block = col // ROWS
+    source = ((block % 8) * 2 + block // 8) * ROWS + col % ROWS
+    return (row == source).astype(F32).astype(BF16)
+
+
+def to_order(x):
+    blocks = [x[ROWS * b : ROWS * (b + 1)] for b in range(NY)]
+    return jnp.concatenate([blocks[(p % 8) * 2 + p // 8] for p in range(NY)], axis=0)
+
+
+def from_order(x):
+    blocks = [x[ROWS * p : ROWS * (p + 1)] for p in range(NY)]
+    return jnp.concatenate([blocks[place(b)] for b in range(NY)], axis=0)
 
 
 def forward(stream, w_t, wo_t, mask, save):
@@ -56,8 +78,8 @@
             powers = jnp.where(mask, powers, 0.0)
         attn = (powers / jnp.sum(powers, axis=0, keepdims=True)).astype(BF16)
         save["attn"][h] = attn
-        mixed.append(dot(val[h], attn, 1, 0).astype(BF16))
-    mixed = jnp.concatenate(mixed, axis=0)
+        mixed.append(dot(val[h], attn, 1, 0))
+    mixed = to_order(jnp.concatenate(mixed, axis=0)).astype(BF16)
     save["inv"][...] = inv
     save["normed"][...] = normed
     save["inv_qk"][...] = inv_qk.reshape(2 * HEADS, 1, TOK)
@@ -69,7 +91,7 @@
 
 
 def backward(grad, w_t, wo_t, save):
-    mixed_grad = dot(grad, wo_t, 1, 0).T.astype(BF16)
+    mixed_grad = from_order(dot(grad, wo_t, 1, 0).T).astype(BF16)
     packed_grad = [None] * (3 * HEADS)
     for h in range(HEADS):
         q, k, v = save["qkv"][h], save["qkv"][HEADS + h], save["qkv"][2 * HEADS + h]
@@ -155,19 +177,29 @@
     return stage[...].astype(BF16)
 
 
-def join_features(parts, layer):
+def join_blocks(parts, pieces, tiles):
     lane = lax.broadcasted_iota(jnp.int32, (CH, 128), 1)
-    tiles = []
-    for t in range(3):
+    joined = []
+    for t in range(tiles):
         tile = None
-        for g in range(NY):
-            start = ROWS * g - 128 * t
+        for n, (g, first) in enumerate(pieces):
+            start = ROWS * n - 128 * t
             if start + ROWS <= 0 or start >= 128:
                 continue
-            piece = pltpu.roll(parts[g], (start - ROWS * layer) % 128, 1)
+            piece = pltpu.roll(parts[g], (start - first) % 128, 1)
             tile = piece if tile is None else jnp.where(lane >= start, piece, tile)
-        tiles.append(tile)
-    return jnp.concatenate(tiles, axis=1)
+        joined.append(tile)
+    return joined
+
+
+def half_roll(x):
+    return pltpu.roll(x, 64, 1)
+
+
+def join_halves(a, b):
+    low = lax.broadcasted_iota(jnp.int32, (CH, 128), 1) < 64
+    b0, b1 = half_roll(b[:, 0:128]), half_roll(b[:, 128:256])
+    return jnp.concatenate([a[:, 0:128], jnp.where(low, a[:, 128:256], b0), jnp.where(low, b0, b1)], axis=1).astype(BF16)
 
 
 def slot_of(unit):
@@ -178,7 +210,8 @@
     for unit in range(NG):
         chunk = gathered[layer, slot_of(unit)].astype(F32)
         stage[QKV * unit : QKV * (unit + 1)] = chunk[:QKV]
-        stage[3 * D + OUT * unit : 3 * D + OUT * (unit + 1)] = chunk[QKV:]
+        at = 3 * D + ROWS * place(unit // 2) + OUT * (unit % 2)
+        stage[at : at + OUT] = chunk[QKV:]
     w_t[layer] = stage[: 3 * D].astype(BF16)
     wo_t[layer] = stage[3 * D :].astype(BF16)
 
@@ -187,16 +220,18 @@
     vol_hbm, cot_hbm, w_hbm, wo_hbm, out,
     vol, w_in, wo_in,
     h1s, h1r, h2s, h2r, h3s, h3r, g3s, g3r, g2s, g2r, g1s, g1r, cotr,
-    wparts, gathered, w_t, wo_t, wstage, cstage,
+    order, wparts, ybuf, gathered, w_t, wo_t, wstage, cstage,
     *rest,
 ):
     saves = []
     for i in range(3):
         a, b, c, d, e = rest[5 * i : 5 * i + 5]
         saves.append(dict(attn=a, inv=b, normed=c, inv_qk=d, qkv=e))
-    load_sems, a2a_send, a2a_recv, cot_send, cot_recv, w_sems, wd_send, wd_recv, wx_recv, wc_send, wc_recv = rest[15:]
+    load_sems, a2a_send, a2a_recv, cot_send, cot_recv, w_sems, y_send, y_recv, x_send, x_first, x_recv, c_send, c_recv = rest[15:]
     gz, gy, gx = lax.axis_index("gz"), lax.axis_index("gy"), lax.axis_index("gx")
     core, ylo = gx % 2, gx // 2
+    z, yhi = gy // 2, gy % 2
+    y = yhi * 4 + ylo
     line = ((gz + NZ - 1) % NZ) * NX + gx
     column = gx * NZ + gz
 
@@ -222,34 +257,36 @@
         pltpu.make_async_copy(ref, ref, sem).wait()
 
     def each(count, body):
-        lax.fori_loop(0, count, lambda k, c: (body(k), c)[1], 0)
+        for k in range(count):
+            body(k)
 
     barrier = pltpu.get_barrier_semaphore()
 
     def greet(to):
         pl.semaphore_signal(barrier, inc=1, device_id=to, device_id_type=MESH)
 
-    each(NY - 1, lambda k: greet((gz, (gy + 1 + k) % NY, gx)))
-
-    def greet_line(k):
-        s = (column + 1 + k) % NG
-        z, x = column_owner(s)
-        greet((z, gy, x))
-
-    each(NG - 1, greet_line)
-    each(NX, lambda k: greet((gy // 4, line // 2, k)))
+    def on_z(k):
+        return gz, ((z + 1 + k) % 8) * 2 + yhi, gx
+
+    def on_y(k):
+        to = (y + 1 + k) % 8
+        return gz, z * 2 + to // 4, (to % 4) * 2 + core
+
+    def on_x(k):
+        return (gz + 1 + k) % NZ, gy, gx
+
+    sibling = (gz, gy, gx + 1 - 2 * core)
+    each(7, lambda k: greet(on_z(k)))
+    each(7, lambda k: greet(on_y(k)))
+    each(3, lambda k: greet(on_x(k)))
+    greet(sibling)
 
     loads[0].wait()
     loads[1].wait()
-    wparts[gy] = own_chunk(w_in, wo_in, cstage)
-    pl.semaphore_wait(barrier, NY - 1 + NG - 1 + 8)
-
-    each(
-        NY - 1,
-        lambda k: send(
-            wparts.at[gy], wparts.at[gy], w_sems.at[0], w_sems.at[1], (gz, (gy + 1 + k) % NY, gx)
-        ),
-    )
+    wparts[z] = own_chunk(w_in, wo_in, cstage)
+    pl.semaphore_wait(barrier, 18)
+
+    each(7, lambda k: send(wparts.at[z], wparts.at[z], w_sems.at[0], w_sems.at[1], on_z(k)))
 
     def gz_exchange(src, dst, n):
         def body(k):
@@ -268,84 +305,83 @@
         pltpu.make_async_copy(src.at[gy], dst.at[gy], a2a_recv.at[n]).start()
 
     loads[2].wait()
-    split_home(vol[...], h1s)
+    order[...] = order_matrix()
+    split_home(dot(vol[...].reshape(TOK, D), order[...], 1, 0).reshape(8, 16, D), h1s)
     gz_exchange(h1s, h1r, 0)
 
-    drain(wparts.at[pl.ds(0, NY - 1)], w_sems.at[1])
+    drain(wparts.at[pl.ds(0, 7)], w_sems.at[1])
     parts = wparts[...].astype(F32)
-    own = gz * 4 + ylo
-    sibling = (gz, gy, gx + 1 - 2 * core)
-
-    def piece(layer, at):
-        return gathered.at[layer, core * 16 + at]
-
-    def run4(layer, z):
-        return gathered.at[layer, pl.ds(core * 16 + z * 4, 4)]
 
     def send_y(layer):
-        def body(k):
-            to = (ylo + 1 + k) % 4
-            block = piece(layer, own)
-            send(block, block, wd_send.at[layer], wd_recv.at[layer, own], (gz, gy, to * 2 + core))
-
-        each(3, body)
+        tiles = join_blocks(parts, [(g, ROWS * layer) for g in range(8)], 2)
+        ybuf[layer, y] = jnp.concatenate(tiles, axis=1).astype(BF16)
+        block = ybuf.at[layer, y]
+        each(7, lambda k: send(block, block, y_send.at[layer], y_recv.at[layer, y], on_y(k)))
+
+    send_y(0)
+
+    def run4(layer, at):
+        return gathered.at[layer, pl.ds(core * 16 + at * 4, 4)]
 
     def send_x(layer, block, sem):
-        each(3, lambda k: send(block, block, wd_send.at[layer], sem, ((gz + 1 + k) % NZ, gy, gx)))
+        each(3, lambda k: send(block, block, x_send.at[layer], sem, on_x(k)))
 
     def send_core(layer, block):
-        send(block, block, wc_send.at[layer], wc_recv.at[layer], sibling)
-
-    gathered[0, core * 16 + own] = join_features(parts, 0).astype(BF16)
-    send_y(0)
-    send_x(0, piece(0, own), wd_recv.at[0, own])
-    send_core(0, piece(0, own))
-    for layer in (1, 2):
-        gathered[layer, core * 16 + own] = join_features(parts, layer).astype(BF16)
+        send(block, block, c_send.at[layer], c_recv.at[layer], sibling)
+
+    def join_y(layer, u):
+        for half in range(2):
+            at = half * 4 + u
+
+            @pl.when(at != y)
+            def _(at=at):
+                drain(ybuf.at[layer, at], y_recv.at[layer, at])
+
+        at = core * 16 + gz * 4 + u
+        gathered[layer, at] = join_halves(ybuf[layer, u].astype(F32), ybuf[layer, 4 + u].astype(F32))
+        return gathered.at[layer, at]
 
     def pass_y(k):
-        at = gz * 4 + (ylo + 1 + k) % 4
-        block = piece(0, at)
-        drain(block, wd_recv.at[0, at])
-        send_x(0, block, wd_recv.at[0, at])
+        u = (ylo + k) % 4
+        block = join_y(0, u)
+        send_x(0, block, x_first.at[gz * 4 + u])
         send_core(0, block)
 
-    each(3, pass_y)
+    each(4, pass_y)
     send_y(1)
-    send_y(2)
 
     def pass_x(k):
         at = ((gz + 1 + k % 3) % NZ) * 4 + (ylo + k // 3) % 4
-        block = piece(0, at)
-        drain(block, wd_recv.at[0, at])
+        block = gathered.at[0, core * 16 + at]
+        drain(block, x_first.at[at])
         send_core(0, block)
 
     each(12, pass_x)
 
     def spread(layer):
-        def wait_y(k):
-            at = gz * 4 + (ylo + 1 + k) % 4
-            drain(piece(layer, at), wd_recv.at[layer, at])
-
-        each(3, wait_y)
+        def body(k):
+            join_y(layer, (ylo + k) % 4)
+
+        each(4, body)
         block = run4(layer, gz)
-        send_x(layer, block, wx_recv.at[layer, gz])
+        send_x(layer, block, x_recv.at[layer - 1, gz])
         send_core(layer, block)
 
     def pass_runs(layer):
         def body(k):
-            z = (gz + 1 + k) % NZ
-            block = run4(layer, z)
-            drain(block, wx_recv.at[layer, z])
+            at = (gz + 1 + k) % NZ
+            block = run4(layer, at)
+            drain(block, x_recv.at[layer - 1, at])
             send_core(layer, block)
 
         each(3, body)
 
     def finish_weights(layer):
-        drain(gathered.at[layer, pl.ds(0, 16)], wc_recv.at[layer])
+        drain(gathered.at[layer, pl.ds(0, 16)], c_recv.at[layer])
         compact(gathered, layer, w_t, wo_t, wstage)
 
     spread(1)
+    send_y(2)
 
     def send_cot(k):
         z, x = line_owner(2 * gy + k % 2)
@@ -396,9 +432,10 @@
     pass_runs(2)
     finish_weights(2)
     drain(cotr, cot_recv)
+    g = dot(cotr[...].reshape(TOK, D), order[...], 1, 0).astype(BF16)
     drain(h3r, a2a_recv.at[2])
     forward(unpack4(h3r), w_t[2], None, None, saves[2])
-    g = backward(cotr[...].reshape(TOK, D), w_t[2], wo_t[2], saves[2])
+    g = backward(g, w_t[2], wo_t[2], saves[2])
     pack4(g, g3s)
     column_exchange(g3s, g3r, 3)
 
@@ -409,15 +446,16 @@
 
     drain(g2r, a2a_recv.at[4])
     g = backward(unpack8(g2r).astype(BF16), w_t[0], wo_t[0], saves[0])
-    g1s[...] = g.astype(BF16).reshape(NZ, 32, D)
+    g1s[...] = dot(g.astype(BF16), order[...], 1, 1).astype(BF16).reshape(NZ, 32, D)
     gz_exchange(g1s, g1r, 5)
 
-    drain(wparts.at[pl.ds(0, NY - 1)], w_sems.at[0])
+    drain(wparts.at[pl.ds(0, 7)], w_sems.at[0])
     drain(h1r.at[pl.ds(0, NZ - 1)], a2a_send.at[0])
     drain(cotr, cot_send)
     for layer in range(3):
-        drain(gathered.at[layer, pl.ds(0, 15)], wd_send.at[layer])
-        drain(gathered.at[layer, pl.ds(0, 16)], wc_send.at[layer])
+        drain(ybuf.at[layer, pl.ds(0, 7)], y_send.at[layer])
+        drain(gathered.at[layer, pl.ds(0, 12)], x_send.at[layer])
+        drain(gathered.at[layer, pl.ds(0, 16)], c_send.at[layer])
     for n, ref in ((1, h2r), (4, g2r)):
         drain(ref.at[pl.ds(0, NY - 1)], a2a_send.at[n])
     for n, ref in ((2, h3r), (3, g3r)):
@@ -449,7 +487,9 @@
         *[vmem((NY, 32, 128), BF16)] * 2,
         *[vmem((NZ, 32, D), BF16)] * 2,
         vmem((NX, 16, D), BF16),
-        vmem((NY, CH, 128), BF16),
+        vmem((D, D), BF16),
+        vmem((8, CH, 128), BF16),
+        vmem((3, 8, CH, 256), BF16),
         vmem((3, NG, CH, D), BF16),
         vmem((3, 3 * D, D), BF16),
         vmem((3, D, D), BF16),
@@ -463,8 +503,10 @@
         dma,
         dma((2,)),
         dma((3,)),
-        dma((3, 16)),
-        dma((3, NZ)),
+        dma((3, 8)),
+        dma((3,)),
+        dma((16,)),
+        dma((2, NZ)),
         dma((3,)),
         dma((3,)),
     ]

time: 85.4 us -> 81.2 us (0.951)
  the two profiles are of different devices: /device:TPU:1 before, /device:TPU:8 now
where the time goes in v3:
time: 81.2 us; the launch traced here: 81 us
  Pallas kernels  79.4 us (98%)
  local copies, waits for them, and re-layouts  1.54 us (2%)
    pallas_call x1, Pallas kernels, local(): pl.pallas_call(kernel, out_shape=jax.ShapeDtypeStruct((8, 16, D), BF16),...  79.4 us

profile of v3, /device:TPU:8, one launch (start us, length us, event | category | flops | bytes accessed | tf_op | source)
XLA Modules:
  0.0 81.0 jit_solution(3955610462327997618)
XLA Ops:
  0.0 79.4 %shard_map.46 = bf16[8,16,384]{2,1,0:T(8,128)(2,1)} custom-call(bf16[8,16,384]{2,1,0:T(8,128)(2,1)} %bitcast.7, bf16[8,16,384]{2,1,0:T(8,128)(2,1)} %bitcast.8, bf16[3,24,36]{2,1,0:T(8,128)(2,1)} %w_hbm.1, bf16[3,12,24]{2,1,0:T(8,128)(2,1)} %bitcast.9), custom_call_target="tpu_custom_call" | custom-call | tf_op jit(solution)/shard_map/pallas_call | solution.py:515
  79.4 1.5 %copy.7 = bf16[8,1,16,384]{3,2,1,0:T(8,128)(2,1)} copy(bf16[8,1,16,384]{3,2,1,0:T(8,128)(2,1)} %bitcast.6) | data formatting | bytes 196608

commit v4 on v3

--- a/solution.py
+++ b/solution.py
@@ -21,6 +21,19 @@
 OUT = 12
 CH = QKV + OUT
 ROWS = 24
+
+
+def ring(d, n):
+    return min(d, n - d)
+
+
+FAR_GY = sorted(
+    ((dz, dy) for dz in range(8) for dy in range(2) if dz or dy), key=lambda p: -(ring(p[0], 8) + 4 * p[1])
+)
+FAR_GX = sorted(
+    ((dx, m, dc) for dx in range(4) for m in range(4) for dc in range(2) if dx or m or dc),
+    key=lambda p: -(ring(p[0], 4) + p[1]),
+)
 
 
 def dot(a, b, ca, cb):
@@ -260,6 +273,11 @@
         for k in range(count):
             body(k)
 
+    def far(k):
+        dx, m, dc = FAR_GX[k]
+        to = (ylo, ylo + 1 - 2 * (ylo % 2), (ylo + 2) % 4, 3 - ylo)[m]
+        return (gz + dx) % NZ, to * 2 + (core + dc) % 2
+
     barrier = pltpu.get_barrier_semaphore()
 
     def greet(to):
@@ -298,7 +316,8 @@
 
     def gy_exchange(src, dst, n):
         def body(k):
-            to = (gy + 1 + k) % NY
+            dz, dy = FAR_GY[k]
+            to = ((z + dz) % 8) * 2 + (yhi + dy) % 2
             send(src.at[to], dst.at[gy], a2a_send.at[n], a2a_recv.at[n], (gz, to, gx))
 
         each(NY - 1, body)
@@ -344,20 +363,26 @@
     def pass_y(k):
         u = (ylo + k) % 4
         block = join_y(0, u)
-        send_x(0, block, x_first.at[gz * 4 + u])
+        for way in (1, 3):
+            send(block, block, x_send.at[0], x_first.at[gz * 4 + u], ((gz + way) % NZ, gy, gx))
         send_core(0, block)
 
-    each(4, pass_y)
-    send_y(1)
-
-    def pass_x(k):
-        at = ((gz + 1 + k % 3) % NZ) * 4 + (ylo + k // 3) % 4
+    for k in range(4):
+        pass_y(k)
+        if k == 1:
+            send_y(1)
+
+    def pass_x(way, k):
+        at = ((gz + way) % NZ) * 4 + (ylo + k) % 4
         block = gathered.at[0, core * 16 + at]
         drain(block, x_first.at[at])
+        if (way, k) in ((3, 0), (3, 1), (1, 2), (1, 3)):
+            send(block, block, x_send.at[0], x_first.at[at], ((gz - way + NZ) % NZ, gy, gx))
         send_core(0, block)
 
-    each(12, pass_x)
-
+    for k in range(4):
+        pass_x(3, k)
+        pass_x(1, k)
     def spread(layer):
         def body(k):
             join_y(layer, (ylo + k) % 4)
@@ -366,6 +391,11 @@
         block = run4(layer, gz)
         send_x(layer, block, x_recv.at[layer - 1, gz])
         send_core(layer, block)
+
+    spread(1)
+    send_y(2)
+    for k in range(4):
+        pass_x(2, k)
 
     def pass_runs(layer):
         def body(k):
@@ -380,8 +410,6 @@
         drain(gathered.at[layer, pl.ds(0, 16)], c_recv.at[layer])
         compact(gathered, layer, w_t, wo_t, wstage)
 
-    spread(1)
-    send_y(2)
 
     def send_cot(k):
         z, x = line_owner(2 * gy + k % 2)
@@ -407,8 +435,8 @@
 
     def line_exchange(src, dst, n):
         def body(k):
-            d = (line + 1 + k) % NG
-            z, x = line_owner(d)
+            z, x = far(k)
+            d = ((z + NZ - 1) % NZ) * NX + x
             send(src.at[d // 2, d % 2], dst.at[column // 2, column % 2], a2a_send.at[n], a2a_recv.at[n], (z, gy, x))
 
         each(NG - 1, body)
@@ -418,8 +446,8 @@
 
     def column_exchange(src, dst, n):
         def body(k):
-            s = (column + 1 + k) % NG
-            z, x = column_owner(s)
+            z, x = far(k)
+            s = x * NZ + z
             send(src.at[s // 2, s % 2], dst.at[line // 2, line % 2], a2a_send.at[n], a2a_recv.at[n], (z, gy, x))
 
         each(NG - 1, body)
@@ -519,13 +547,18 @@
         out_specs=whole,
         scratch_shapes=scratch,
         compiler_params=pltpu.CompilerParams(
-            collective_id=0, has_side_effects=True, vmem_limit_bytes=63_400_000
+            collective_id=0, has_side_effects=True, vmem_limit_bytes=50_000_000
         ),
     )(
-        volume.reshape(8, 16, D),
-        cotangent.reshape(8, 16, D),
-        w_project,
-        jnp.swapaxes(w_output, 1, 2),
+        *(
+            pltpu.with_memory_space_constraint(array, pltpu.HBM)
+            for array in (
+                volume.reshape(8, 16, D),
+                cotangent.reshape(8, 16, D),
+                w_project,
+                jnp.swapaxes(w_output, 1, 2),
+            )
+        )
     )
     return got.reshape(block)
 

time: 81.2 us -> 78 us (0.961)
  the two profiles are of different devices: /device:TPU:8 before, /device:TPU:1 now
where the time goes in v4:
time: 78 us; the launch traced here: 77 us
  Pallas kernels  76.4 us (98%)
    pallas_call x1, Pallas kernels, local(): pl.pallas_call(kernel, out_shape=jax.ShapeDtypeStruct((8, 16, D), BF16),...  76.4 us

profile of v4, /device:TPU:1, one launch (start us, length us, event | category | flops | bytes accessed | tf_op | source)
XLA Modules:
  0.0 77.0 jit_solution(15432865564989187252)
XLA Ops:
  0.0 76.4 %shard_map.46 = bf16[8,16,384]{2,1,0:T(8,128)(2,1)S(1)} custom-call(bf16[8,16,384]{2,1,0:T(8,128)(2,1)} %bitcast.7, bf16[8,16,384]{2,1,0:T(8,128)(2,1)} %bitcast.8, bf16[3,24,36]{2,1,0:T(8,128)(2,1)} %w_hbm.1, bf16[3,12,24]{2,1,0:T(8,128)(2,1)} %bitcast.9), custom_call_target="tpu_custom_call" | custom-call | tf_op jit(solution)/shard_map/pallas_call | solution.py:543
  76.4 0.6 copy.7

commit v5 on v4

--- a/solution.py
+++ b/solution.py
@@ -83,45 +83,47 @@
     inv_qk = lax.rsqrt(jnp.mean(heads[:2] * heads[:2], axis=2, keepdims=True) + EPS)
     qk = (heads[:2] * inv_qk).astype(BF16)
     val = heads[2].astype(BF16)
-    mixed = []
-    for h in range(HEADS):
-        scores = dot(qk[1, h], qk[0, h], 0, 0) * (HEAD**-0.5)
-        powers = jnp.exp(scores)
-        if mask is not None:
-            powers = jnp.where(mask, powers, 0.0)
-        attn = (powers / jnp.sum(powers, axis=0, keepdims=True)).astype(BF16)
-        save["attn"][h] = attn
-        mixed.append(dot(val[h], attn, 1, 0))
-    mixed = to_order(jnp.concatenate(mixed, axis=0)).astype(BF16)
+    each_head = range(HEADS)
+    scores = [dot(qk[1, h], qk[0, h], 0, 0) * (HEAD**-0.5) for h in each_head]
+    powers = [jnp.exp(x) for x in scores]
+    if mask is not None:
+        powers = [jnp.where(mask, x, 0.0) for x in powers]
+    attn = [(x / jnp.sum(x, axis=0, keepdims=True)).astype(BF16) for x in powers]
+    mixed = jnp.concatenate([dot(val[h], attn[h], 1, 0) for h in each_head], axis=0)
+    result = None
+    if wo_t is not None:
+        result = stream + dot(wo_t, to_order(mixed).astype(BF16), 1, 0).T
+    for h in each_head:
+        save["attn"][h] = attn[h]
     save["inv"][...] = inv
     save["normed"][...] = normed
     save["inv_qk"][...] = inv_qk.reshape(2 * HEADS, 1, TOK)
     save["qkv"][: 2 * HEADS] = qk.reshape(2 * HEADS, HEAD, TOK)
     save["qkv"][2 * HEADS :] = val
-    if wo_t is None:
-        return None
-    return stream + dot(wo_t, mixed, 1, 0).T
+    return result
 
 
 def backward(grad, w_t, wo_t, save):
     mixed_grad = from_order(dot(grad, wo_t, 1, 0).T).astype(BF16)
-    packed_grad = [None] * (3 * HEADS)
-    for h in range(HEADS):
-        q, k, v = save["qkv"][h], save["qkv"][HEADS + h], save["qkv"][2 * HEADS + h]
-        attn = save["attn"][h]
-        attn32 = attn.astype(F32)
-        d_mixed = mixed_grad[h * HEAD : (h + 1) * HEAD]
-        d_attn = dot(v, d_mixed, 0, 0)
-        d_v = dot(d_mixed, attn, 1, 1)
-        d_scores = attn32 * (d_attn - jnp.sum(d_attn * attn32, axis=0, keepdims=True))
-        d_scores = (d_scores * (HEAD**-0.5)).astype(BF16)
-        d_q = dot(k, d_scores, 1, 0)
-        d_k = dot(q, d_scores, 1, 1)
-        for at, unit, d_unit in ((h, q, d_q), (HEADS + h, k, d_k)):
-            unit32 = unit.astype(F32)
-            proj = jnp.mean(d_unit * unit32, axis=0, keepdims=True)
-            packed_grad[at] = (save["inv_qk"][at] * (d_unit - unit32 * proj)).astype(BF16)
-        packed_grad[2 * HEADS + h] = d_v.astype(BF16)
+    each_head = range(HEADS)
+    q, k, v = ([save["qkv"][HEADS * i + h] for h in each_head] for i in range(3))
+    attn = [save["attn"][h] for h in each_head]
+    d_mixed = [mixed_grad[h * HEAD : (h + 1) * HEAD] for h in each_head]
+    d_attn = [dot(v[h], d_mixed[h], 0, 0) for h in each_head]
+    d_v = [dot(d_mixed[h], attn[h], 1, 1).astype(BF16) for h in each_head]
+    d_scores = []
+    for h in each_head:
+        attn32 = attn[h].astype(F32)
+        change = attn32 * (d_attn[h] - jnp.sum(d_attn[h] * attn32, axis=0, keepdims=True))
+        d_scores.append((change * (HEAD**-0.5)).astype(BF16))
+    d_q = [dot(k[h], d_scores[h], 1, 0) for h in each_head]
+    d_k = [dot(q[h], d_scores[h], 1, 1) for h in each_head]
+    packed_grad = []
+    for at, (unit, d_unit) in enumerate(zip(q + k, d_q + d_k)):
+        unit32 = unit.astype(F32)
+        proj = jnp.mean(d_unit * unit32, axis=0, keepdims=True)
+        packed_grad.append((save["inv_qk"][at] * (d_unit - unit32 * proj)).astype(BF16))
+    packed_grad += d_v
     packed_grad = jnp.concatenate(packed_grad, axis=0)
     d_normed = dot(packed_grad, w_t, 0, 0)
     normed32 = save["normed"][...].astype(F32)

time: 78 us -> 75.7 us (0.971)
  Pallas kernels: 76.4 us -> 74.6 us
    pallas_call x1, Pallas kernels: 76.4 us -> 74.6 us  [local(): pl.pallas_call(kernel, out_shape=jax.ShapeDtypeStruct((8, 16, D), BF16),...]
where the time goes in v5:
time: 75.7 us; the launch traced here: 75.2 us
  Pallas kernels  74.6 us (99%)
    pallas_call x1, Pallas kernels, local(): pl.pallas_call(kernel, out_shape=jax.ShapeDtypeStruct((8, 16, D), BF16),...  74.6 us

profile of v5, /device:TPU:1, one launch (start us, length us, event | category | flops | bytes accessed | tf_op | source)
XLA Modules:
  0.0 75.2 jit_solution(6034289126393941076)
XLA Ops:
  0.0 74.6 %shard_map.46 = bf16[8,16,384]{2,1,0:T(8,128)(2,1)S(1)} custom-call(bf16[8,16,384]{2,1,0:T(8,128)(2,1)} %bitcast.7, bf16[8,16,384]{2,1,0:T(8,128)(2,1)} %bitcast.8, bf16[3,24,36]{2,1,0:T(8,128)(2,1)} %w_hbm.1, bf16[3,12,24]{2,1,0:T(8,128)(2,1)} %bitcast.9), custom_call_target="tpu_custom_call" | custom-call | tf_op jit(solution)/shard_map/pallas_call | solution.py:545
  74.6 0.6 copy.7

commit v6 on v5

--- a/solution.py
+++ b/solution.py
@@ -103,8 +103,11 @@
     return result
 
 
-def backward(grad, w_t, wo_t, save):
-    mixed_grad = from_order(dot(grad, wo_t, 1, 0).T).astype(BF16)
+def grad_of_mixed(grad, wo_t):
+    return from_order(dot(grad, wo_t, 1, 0).T).astype(BF16)
+
+
+def backward(grad, w_t, mixed_grad, save):
     each_head = range(HEADS)
     q, k, v = ([save["qkv"][HEADS * i + h] for h in each_head] for i in range(3))
     attn = [save["attn"][h] for h in each_head]
@@ -463,21 +466,18 @@
     finish_weights(2)
     drain(cotr, cot_recv)
     g = dot(cotr[...].reshape(TOK, D), order[...], 1, 0).astype(BF16)
+    mixed_grad = grad_of_mixed(g, wo_t[2])
     drain(h3r, a2a_recv.at[2])
     forward(unpack4(h3r), w_t[2], None, None, saves[2])
-    g = backward(g, w_t[2], wo_t[2], saves[2])
+    g = backward(g, w_t[2], mixed_grad, saves[2])
     pack4(g, g3s)
     column_exchange(g3s, g3r, 3)
 
     drain(g3r, a2a_recv.at[3])
-    g = backward(unpack4(g3r).astype(BF16), w_t[1], wo_t[1], saves[1])
+    g = unpack4(g3r).astype(BF16)
+    g = backward(g, w_t[1], grad_of_mixed(g, wo_t[1]), saves[1])
     pack8(g, g2s)
     gy_exchange(g2s, g2r, 4)
-
-    drain(g2r, a2a_recv.at[4])
-    g = backward(unpack8(g2r).astype(BF16), w_t[0], wo_t[0], saves[0])
-    g1s[...] = dot(g.astype(BF16), order[...], 1, 1).astype(BF16).reshape(NZ, 32, D)
-    gz_exchange(g1s, g1r, 5)
 
     drain(wparts.at[pl.ds(0, 7)], w_sems.at[0])
     drain(h1r.at[pl.ds(0, NZ - 1)], a2a_send.at[0])
@@ -491,8 +491,13 @@
     for n, ref in ((2, h3r), (3, g3r)):
         drain(ref.at[pl.ds(0, 15)], a2a_send.at[n])
         drain(ref.at[15, pl.ds(0, 1)], a2a_send.at[n])
+    drain(g2r, a2a_recv.at[4])
+    g = unpack8(g2r).astype(BF16)
+    g = backward(g, w_t[0], grad_of_mixed(g, wo_t[0]), saves[0])
+    g1s[...] = dot(g.astype(BF16), order[...], 1, 1).astype(BF16).reshape(NZ, 32, D)
+    gz_exchange(g1s, g1r, 5)
+
     drain(g1r.at[pl.ds(0, NZ - 1)], a2a_send.at[5])
-
     drain(g1r, a2a_recv.at[5])
     join_home(g1r, out)
 

time: 75.7 us -> 75.4 us (level)
  no operation moved by 1% of the time
where the time goes in v6:
time: 75.4 us; the launch traced here: 75 us
  Pallas kernels  74.3 us (99%)
    pallas_call x1, Pallas kernels, local(): pl.pallas_call(kernel, out_shape=jax.ShapeDtypeStruct((8, 16, D), BF16),...  74.3 us

profile of v6, /device:TPU:1, one launch (start us, length us, event | category | flops | bytes accessed | tf_op | source)
XLA Modules:
  0.0 75.0 jit_solution(17940307556236263929)
XLA Ops:
  0.0 74.3 %shard_map.46 = bf16[8,16,384]{2,1,0:T(8,128)(2,1)S(1)} custom-call(bf16[8,16,384]{2,1,0:T(8,128)(2,1)} %bitcast.7, bf16[8,16,384]{2,1,0:T(8,128)(2,1)} %bitcast.8, bf16[3,24,36]{2,1,0:T(8,128)(2,1)} %w_hbm.1, bf16[3,12,24]{2,1,0:T(8,128)(2,1)} %bitcast.9), custom_call_target="tpu_custom_call" | custom-call | tf_op jit(solution)/shard_map/pallas_call | solution.py:550
  74.3 0.6 copy.7

commit v7 on v6

--- a/solution.py
+++ b/solution.py
@@ -416,12 +416,6 @@
         compact(gathered, layer, w_t, wo_t, wstage)
 
 
-    def send_cot(k):
-        z, x = line_owner(2 * gy + k % 2)
-        send(cot_hbm.at[k], cotr.at[gx], cot_send, cot_recv, (z, 4 * gz + k // 2, x))
-
-    each(8, send_cot)
-
     finish_weights(0)
     drain(h1r, a2a_recv.at[0])
     depth_mask = line_mask(4)
@@ -433,6 +427,12 @@
     spread(2)
     pass_runs(1)
     finish_weights(1)
+    def send_cot(k):
+        z, x = line_owner(2 * gy + k % 2)
+        send(cot_hbm.at[k], cotr.at[gx], cot_send, cot_recv, (z, 4 * gz + k // 2, x))
+
+    each(8, send_cot)
+
     drain(h2r, a2a_recv.at[1])
     row_mask = line_mask(8)
     x = forward(unpack8(h2r), w_t[1], wo_t[1], row_mask, saves[1])

time: 75.4 us -> 77 us (1.021)
  Pallas kernels: 74.3 us -> 75.2 us
    pallas_call x1, Pallas kernels: 74.3 us -> 75.2 us  [local(): pl.pallas_call(kernel, out_shape=jax.ShapeDtypeStruct((8, 16, D), BF16),...]
where the time goes in v7:
time: 77 us; the launch traced here: 75.8 us
  Pallas kernels  75.2 us (98%)
    pallas_call x1, Pallas kernels, local(): pl.pallas_call(kernel, out_shape=jax.ShapeDtypeStruct((8, 16, D), BF16),...  75.2 us

profile of v7, /device:TPU:1, one launch (start us, length us, event | category | flops | bytes accessed | tf_op | source)
XLA Modules:
  0.0 75.8 jit_solution(1067285880890129389)
XLA Ops:
  0.0 75.2 %shard_map.46 = bf16[8,16,384]{2,1,0:T(8,128)(2,1)S(1)} custom-call(bf16[8,16,384]{2,1,0:T(8,128)(2,1)} %bitcast.7, bf16[8,16,384]{2,1,0:T(8,128)(2,1)} %bitcast.8, bf16[3,24,36]{2,1,0:T(8,128)(2,1)} %w_hbm.1, bf16[3,12,24]{2,1,0:T(8,128)(2,1)} %bitcast.9), custom_call_target="tpu_custom_call" | custom-call | tf_op jit(solution)/shard_map/pallas_call | solution.py:550
  75.2 0.6 copy.7
